TPU v7x, 256 devices: a whole 4x4x8 slice. The times are simulated.
256 devices in a mesh: tm: 8 (over y, core), space: 32 (over z, x).
Axes of the slice: x: 4, y: 4, z: 8, core: 2. Of those that a mesh axis runs over, the one named last changes fastest.
Arguments:
- data: bfloat16 [16384, 32768], P('tm', 'space'), may hold values from -70 to 70, as said below
Outputs:
- rfac: float32 [16, 128, 128], replicated
- modes_t: float32 [16, 128, 32768], P(None, None, ('space', 'tm'))
Inputs may be any that keep to these rules, and one draw needn't show every extreme that they name: `data`: finite values of order one to some tens.
All inputs are finite; a program needn't handle non-finite values.
Results may differ from a plain program's by a relative error of at most 0.0023.
The roundings to bfloat16 on the way count: a program that leaves them out, or rounds other values in their place, can miss the bound.
Values may be sent and summed in bfloat16 or wider, within the bound.
A program may use at most 128 MiB of HBM per device.

v0:
```python
import jax
import jax.numpy as jnp
from jax import lax
from jax.sharding import PartitionSpec as P

NFFT = 256
NB = 64
F = 16
NT = 16384


def make_table():
    steps = jnp.arange(NFFT, dtype=jnp.int32)
    window = 0.5 - 0.5 * jnp.cos(2.0 * jnp.pi * steps.astype(jnp.float32) / NFFT)
    factor = 1.0 / jnp.sqrt(jnp.sum(window * window))
    freqs = jnp.arange(1, F + 1, dtype=jnp.int32)
    phases = (steps[:, None] * freqs[None, :] % NFFT).astype(jnp.float32) * (2.0 * jnp.pi / NFFT)
    table = (
        jnp.concatenate([jnp.cos(phases), -jnp.sin(phases)], axis=1) * (factor * window)[:, None]
    )
    return table.astype(jnp.bfloat16)


def arrange(spectra):
    blocks, width, points = spectra.shape
    return (
        spectra.reshape(blocks, 2, F, points).transpose(2, 1, 0, 3).reshape(F, 2 * blocks, points)
    )


def shards(data):
    n_tm = lax.axis_size("tm")
    n_space = lax.axis_size("space")
    local_times, columns = data.shape
    points = columns // n_tm
    total_points = points * n_tm * n_space
    table = make_table()
    colsum = jnp.sum(table.astype(jnp.float32), axis=0)
    cube = data.reshape(local_times, n_tm, points)
    series = lax.all_to_all(cube, "tm", split_axis=1, concat_axis=0, tiled=True)[:, 0, :]
    count = series.shape[1]
    mean = jnp.sum(series, axis=0, dtype=jnp.float32) / NT
    blocks = series.reshape(NB, NFFT, count)
    spectra = jnp.einsum("kj,bkx->bjx", table, blocks, preferred_element_type=jnp.float32)
    spectra = spectra - colsum[None, :, None] * mean[None, None, :]
    matrix_t = arrange(spectra)
    local_gram = (
        jnp.einsum("fcx,fdx->fcd", matrix_t, matrix_t, precision=lax.Precision.HIGHEST)
        / total_points
    )
    gram = lax.psum(local_gram, ("tm", "space"))
    lower = jnp.linalg.cholesky(gram)
    modes_t = lax.linalg.triangular_solve(lower, matrix_t, left_side=True, lower=True)
    return (jnp.transpose(lower, (0, 2, 1)), modes_t)


def solution(mesh):
    return jax.shard_map(
        shards,
        mesh=mesh,
        in_specs=(P("tm", "space"),),
        out_specs=(P(), P(None, None, ("space", "tm"))),
        check_vma=False,
    )
```

profile of v0, /device:TPU:1, one launch (start us, length us, event | category | flops | bytes accessed | tf_op | source)
XLA Modules:
  0.0 694.9 jit_solution(1532690326269378301)
XLA Ops:
  7.2 4.9 copy_bitcast_fusion
  12.1 7.7 %all-to-all-start = ((bf16[2048,8,128]{2,0,1:T(8,128)(2,1)}), bf16[2048,8,128]{2,0,1:T(8,128)(2,1)}, u32[]{:S(2)}, u32[]{:S(2)}) async-start(bf16[2048,8,128]{2,0,1:T(8,128)(2,1)} %copy_bitcast_fusion), calls=%async_computation | async-start | bytes 8388608 | tf_op jit(solution)/shard_map/all_to_all | solution.py:40
  19.7 0.0 all-reduce.2.cloned.1.call-start
  19.7 0.6 multiply_reduce_fusion
  21.1 0.2 fusion.12
  21.3 0.1 convert_reduce_fusion.1
  21.4 47.3 %all-to-all-done = bf16[2048,8,128]{2,0,1:T(8,128)(2,1)} async-done(((bf16[2048,8,128]{2,0,1:T(8,128)(2,1)}), bf16[2048,8,128]{2,0,1:T(8,128)(2,1)}, u32[]{:S(2)}, u32[]{:S(2)}) %all-to-all-start) | async-done | bytes 4194336 | tf_op jit(solution)/shard_map/all_to_all | solution.py:40
  68.7 4.4 convert_reduce_fusion
  73.0 0.1 broadcast_multiply_fusion
  73.1 3.0 convolution_subtract_fusion
  76.1 0.6 copy.10
  76.7 3.3 convolution_multiply_fusion
  80.0 0.0 all-reduce.2.cloned.1.call-update
  80.1 254.0 %all-reduce.2.cloned.1.call-done = f32[16,128,128]{1,2,0:T(8,128)} async-done(((f32[16,128,128]{1,2,0:T(8,128)}), f32[16,128,128]{1,2,0:T(8,128)}) %all-reduce.2.cloned.1.call-update) | async-done | bytes 1048592 | tf_op jit(solution)/shard_map/psum | solution.py:51
  334.1 1.6 copy.12
  335.7 1.3 fusion.2
  337.0 187.5 %custom-call.7 = f32[16,128,128]{2,1,0:T(8,128)S(1)} custom-call(f32[16,128,128]{2,1,0:T(8,128)S(1)} %fusion.2), custom_call_target="Cholesky" | custom-call | tf_op jit(solution)/shard_map/jit(cholesky)/cholesky | solution.py:52
  524.6 0.1 select_reduce_fusion
  524.7 0.1 compare_reduce_fusion
  524.8 1.2 select_bitcast_fusion
  526.0 1.3 copy.14
  527.3 157.9 %custom-call.8 = f32[16,1,128,128]{2,3,1,0:T(8,128)S(1)} custom-call(f32[16,1,128,128]{3,2,1,0:T(8,128)} %get-tuple-element.6), custom_call_target="InvertDiagBlocksLowerTriangular" | custom-call | tf_op jit(solution)/shard_map/triangular_solve | solution.py:53
  685.2 2.8 fusion
  (5 shorter events, 0.1 us)
Async XLA Ops:
  12.1 56.6 %all-to-all-start = ((bf16[2048,8,128]{2,0,1:T(8,128)(2,1)}), bf16[2048,8,128]{2,0,1:T(8,128)(2,1)}, u32[]{:S(2)}, u32[]{:S(2)}) async-start(bf16[2048,8,128]{2,0,1:T(8,128)(2,1)} %copy_bitcast_fusion), calls=%async_computation | async-start | bytes 8388608 | tf_op jit(solution)/shard_map/all_to_all | solution.py:40
  19.7 314.4 %all-reduce.2.cloned.1.call-start = ((), (), s32[]{:S(2)}) async-start(), calls=%async_computation.1 | async-start | bytes 2097152 | tf_op jit(solution)/shard_map/psum | solution.py:51
Sparse Core Ops, SparseCore 0:
  80.2 253.9 all-reduce.1
where the time goes:
time: 696 us; the launch traced here: 695 us
  other arithmetic  354 us (51%)
  waiting for transfers between devices  301 us (43%)
  between operations  14.8 us (2%)
  matrix products  9.09 us (1%)
  local copies, waits for them, and re-layouts  8.39 us (1%)
  starting transfers between devices  7.66 us (1%)
    psum x1, waiting for transfers between devices, shards(): gram = lax.psum(local_gram, ('tm', 'space'))  254 us
    another operation x4, other arithmetic, shards(): lower = jnp.linalg.cholesky(gram)  188 us
    another operation x2, other arithmetic, shards(): lax.linalg.triangular_solve(lower, matrix_t, left_side=True, lower=True)  159 us
    all_to_all x1, waiting for transfers between devices, shards(): lax.all_to_all(cube, 'tm', split_axis=1, concat_axis=0, tiled=True)[:, 0, :]  47.3 us
  transfers between devices with their start and end apart: 2, of which 2 were waited for; matrix products, arithmetic and copies ran while one was open for 0% of the time, Pallas kernels for 0%

commit v1 on v0

v1 whole, which is shorter than its diff:
```python
import functools

import jax
import jax.numpy as jnp
import ml_dtypes
import numpy as np
from jax import lax
from jax.experimental import pallas as pl
from jax.experimental.pallas import tpu as pltpu
from jax.sharding import PartitionSpec as P

NFFT = 256
NB = 64
F = 16
NT = 16384
NX = 32768
NTM = 8
NSPACE = 32
LB = NB // NTM
COLS = NX // NSPACE
PTS = COLS // NTM
CHUNKS = 4
CW = COLS // CHUNKS
MESH = pl.DeviceIdType.MESH


def make_table():
    steps = np.arange(NFFT)
    window = 0.5 - 0.5 * np.cos(2.0 * np.pi * steps / NFFT)
    factor = 1.0 / np.sqrt(np.sum(window * window))
    freqs = np.arange(1, F + 1)
    phases = (steps[:, None] * freqs[None, :] % NFFT) * (2.0 * np.pi / NFFT)
    real = np.cos(phases) * (factor * window)[:, None]
    imag = -np.sin(phases) * (factor * window)[:, None]
    pairs = np.stack([real.T, imag.T], axis=1).reshape(2 * F, NFFT)
    rounded = pairs.astype(np.float32).astype(ml_dtypes.bfloat16)
    colsum = rounded.astype(np.float32).sum(axis=1, dtype=np.float32)
    rows = np.zeros((48, NFFT), ml_dtypes.bfloat16)
    rows[: 2 * F] = rounded
    rows[2 * F] = 1.0
    return rows, colsum


def factor(gt_ref, w_ref):
    lane = lax.broadcasted_iota(jnp.int32, (8, 128), 1)
    sub = lax.broadcasted_iota(jnp.int32, (8, 128), 0)
    for j in range(16):
        w_ref[j] = gt_ref[j]
    for k in range(16):
        base = 8 * k
        own = w_ref[k]
        cols = [jnp.broadcast_to(own[:, base + i : base + i + 1], (8, 128)) for i in range(8)]
        pivot_rows, inverses, cross = [], [], []
        diag = jnp.ones((8, 128), jnp.float32)
        for i in range(8):
            d = jnp.broadcast_to(cols[i][i : i + 1, :], (8, 128))
            inv = 1.0 / d
            row = jnp.broadcast_to(own[i : i + 1, :], (8, 128))
            diag = jnp.where(sub == i, d, diag)
            f = jnp.where(sub > i, cols[i] * inv, 0.0)
            here = [jnp.broadcast_to(cols[m][i : i + 1, :], (8, 128)) for m in range(i + 1, 8)]
            for n, m in enumerate(range(i + 1, 8)):
                cols[m] = cols[m] - f * here[n]
            unit = jnp.where(lane == base + i, 1.0, row)
            own = jnp.where((lane == base + i) & (sub > i), 0.0, own) - f * unit
            pivot_rows.append(jnp.where((lane > base + i) & (lane < base + 8), 0.0, unit))
            inverses.append(inv)
            cross.append(here)
        w_ref[k] = own * lax.rsqrt(diag)
        for j in range(k + 1, 16):
            rest = w_ref[j]
            mult = [jnp.broadcast_to(rest[:, base + i : base + i + 1], (8, 128)) for i in range(8)]
            rest = jnp.where((lane >= base) & (lane < base + 8), 0.0, rest)
            for i in range(8):
                f = mult[i] * inverses[i]
                for n, m in enumerate(range(i + 1, 8)):
                    mult[m] = mult[m] - f * cross[i][n]
                rest = rest - f * pivot_rows[i]
            w_ref[j] = rest


def main_kernel(
    data, tab, cs, wa, mf,
    dbuf, spec, sb, rb, ls, mat, gs, gr, gt, w,
    load_sem, fs_sem, fr_sem, ls_ssem, ls_rsem, ps_sem, pr_sem,
    ga_ssem, ga_rsem, gb_ssem, gb_rsem, w_ssem, w_rsem, own_sem,
):
    t = lax.axis_index("tm")
    s = lax.axis_index("space")
    z, x = s // 4, s % 4
    h = x % 2
    tile = (x // 2) * 8 + z
    pair = z * 4 + (x // 2) * 2

    loads = []
    for c in range(CHUNKS):
        copy = pltpu.make_async_copy(
            data.at[:, pl.ds(c * CW, CW)], dbuf.at[c], load_sem.at[c]
        )
        copy.start()
        loads.append(copy)

    barrier = pltpu.get_barrier_semaphore()

    def greet_tm(k, carry):
        other = (t + k) % NTM
        pl.semaphore_signal(barrier, inc=1, device_id=(other, s), device_id_type=MESH)
        pl.semaphore_signal(
            barrier, inc=1, device_id=(other, pair + 1 - h), device_id_type=MESH
        )
        return carry

    def greet_space(k, carry):
        pl.semaphore_signal(
            barrier, inc=1, device_id=(t, (s + k) % NSPACE), device_id_type=MESH
        )
        return carry

    lax.fori_loop(1, NTM, greet_tm, 0)
    lax.fori_loop(1, NSPACE, greet_space, 0)

    def freq_copy(c, other):
        cols = pl.ds(c * CW, CW)
        return pltpu.make_async_remote_copy(
            src_ref=sb.at[pl.ds(2 * other, 2), :, cols],
            dst_ref=rb.at[:, pl.ds(t * 16, 16), cols],
            send_sem=fs_sem.at[c, other],
            recv_sem=fr_sem.at[c, t],
            device_id=(other, s),
            device_id_type=MESH,
        )

    for c in range(CHUNKS):
        cols = pl.ds(c * CW, CW)
        loads[c].wait()
        total = jnp.zeros((1, CW), jnp.float32)
        for b in range(LB):
            out = jnp.dot(
                tab[...], dbuf[c, pl.ds(b * NFFT, NFFT), :], preferred_element_type=jnp.float32
            )
            for r in range(CW // 128):
                spec[c * (CW // 128) + r, pl.ds(b, 2 * F, stride=LB), :] = out[
                    : 2 * F, r * 128 : (r + 1) * 128
                ]
            total = total + out[2 * F : 2 * F + 1]
        for r in range(CW // 128):
            ls[t, pl.ds(c * (CW // 128) + r, 1), :] = total[:, r * 128 : (r + 1) * 128]
        local_mean = jnp.broadcast_to(total * (NTM / NT), (LB, CW))
        for r in range(CW // 128):
            place = c * (CW // 128) + r
            for f in range(F):
                parts = [
                    spec[place, pl.ds(f * 16 + ri * 8, 8), :]
                    - cs[2 * f + ri] * local_mean[:, r * 128 : (r + 1) * 128]
                    for ri in range(2)
                ]
                sb[f, :, pl.ds(place * 128, 128)] = jnp.concatenate(parts, axis=0).astype(
                    jnp.bfloat16
                )
        if c == 0:
            pl.semaphore_wait(barrier, 2 * (NTM - 1) + NSPACE - 1)

        def send(k, carry):
            freq_copy(c, (t + k) % NTM).start()
            return carry

        lax.fori_loop(1, NTM, send, 0)

    def sum_copy(other):
        return pltpu.make_async_remote_copy(
            src_ref=ls.at[t],
            dst_ref=ls.at[t],
            send_sem=ls_ssem.at[other],
            recv_sem=ls_rsem.at[t],
            device_id=(other, s),
            device_id_type=MESH,
        )

    def send_sums(k, carry):
        sum_copy((t + k) % NTM).start()
        return carry

    lax.fori_loop(1, NTM, send_sums, 0)
    for f2 in range(2):
        rb[f2, pl.ds(t * 16, 16), :] = sb[2 * t + f2]

    def recv_sums(k, carry):
        other = (t + k) % NTM
        pltpu.make_async_remote_copy(
            src_ref=ls.at[t],
            dst_ref=ls.at[other],
            send_sem=ls_ssem.at[other],
            recv_sem=ls_rsem.at[other],
            device_id=(other, s),
            device_id_type=MESH,
        ).wait()
        return carry

    lax.fori_loop(1, NTM, recv_sums, 0)
    mean = ls[0]
    for k in range(1, NTM):
        mean = mean + ls[k]
    mean = mean * (1.0 / NT)

    def subtract(f, carry):
        for ri in range(2):
            rows = pl.ds(pl.multiple_of(f * 16 + ri * 8, 8), 8)
            for r in range(8):
                spec[r, rows, :] = spec[r, rows, :] - cs[2 * f + ri] * mean[r : r + 1, :]
        return carry

    lax.fori_loop(0, F, subtract, 0)

    def point_copy(other):
        return pltpu.make_async_remote_copy(
            src_ref=spec5.at[other],
            dst_ref=mf.at[:, :, t],
            send_sem=ps_sem.at[other],
            recv_sem=pr_sem.at[t],
            device_id=(other, s),
            device_id_type=MESH,
        )

    spec5 = spec.reshape(NTM, F, 2, LB, PTS)

    def send_points(k, carry):
        point_copy((t + k) % NTM).start()
        return carry

    lax.fori_loop(1, NTM, send_points, 0)
    own_points = pltpu.make_async_copy(
        spec5.at[t], mf.at[:, :, t], own_sem
    )
    own_points.start()

    def recv_freq(k, carry):
        other = (t + k) % NTM
        for c in range(CHUNKS):
            cols = pl.ds(c * CW, CW)
            pltpu.make_async_remote_copy(
                src_ref=sb.at[pl.ds(2 * other, 2), :, cols],
                dst_ref=rb.at[:, pl.ds(other * 16, 16), cols],
                send_sem=fs_sem.at[c, other],
                recv_sem=fr_sem.at[c, other],
                device_id=(other, s),
                device_id_type=MESH,
            ).wait()
        return carry

    lax.fori_loop(1, NTM, recv_freq, 0)
    for f2 in range(2):
        real, imag = cs[4 * t + 2 * f2], cs[4 * t + 2 * f2 + 1]

        def gather(k, carry):
            shift = ls[k] * (NTM / NT) - mean
            for r in range(8):
                lanes = pl.ds(r * 128, 128)
                block = rb[f2, pl.ds(pl.multiple_of(k * 16, 16), 16), lanes].astype(jnp.float32)
                row = jnp.broadcast_to(shift[r : r + 1, :], (8, 128))
                mat[pl.ds(pl.multiple_of(k * 8, 8), 8), lanes] = block[:8] + real * row
                mat[pl.ds(pl.multiple_of(64 + k * 8, 8), 8), lanes] = block[8:] + imag * row
            return carry

        lax.fori_loop(0, NTM, gather, 0)
        rounded = mat[...].astype(jnp.bfloat16)
        gram = lax.dot_general(
            rounded, rounded, (((1,), (1,)), ((), ())), preferred_element_type=jnp.float32
        ) * (1.0 / NX)
        for i in range(16):
            gs[f2, i] = gram[i * 8 : (i + 1) * 8]

    def gram_copy(k):
        other = (s + k) % NSPACE
        ox, oz = other % 4, other // 4
        return pltpu.make_async_remote_copy(
            src_ref=gs.at[ox % 2, (ox // 2) * 8 + oz],
            dst_ref=gr.at[s],
            send_sem=ga_ssem.at[other],
            recv_sem=ga_rsem.at[s],
            device_id=(t, other),
            device_id_type=MESH,
        )

    def send_gram(k, carry):
        gram_copy(k).start()
        return carry

    lax.fori_loop(1, NSPACE, send_gram, 0)
    gr[s] = gs[h, tile]

    def recv_gram(k, carry):
        other = (s + k) % NSPACE
        ox, oz = other % 4, other // 4
        pltpu.make_async_remote_copy(
            src_ref=gs.at[ox % 2, (ox // 2) * 8 + oz],
            dst_ref=gr.at[other],
            send_sem=ga_ssem.at[other],
            recv_sem=ga_rsem.at[other],
            device_id=(t, other),
            device_id_type=MESH,
        ).wait()
        return carry

    lax.fori_loop(1, NSPACE, recv_gram, 0)
    rows = gr[0]
    for k in range(1, NSPACE):
        rows = rows + gr[k]
    gt[tile] = rows

    def tile_copy(k, landing):
        other = (tile + k) % 16
        ox, oz = (other // 8) * 2 + h, other % 8
        return pltpu.make_async_remote_copy(
            src_ref=gt.at[tile],
            dst_ref=gt.at[other if landing else tile],
            send_sem=gb_ssem.at[other],
            recv_sem=gb_rsem.at[other if landing else tile],
            device_id=(t, oz * 4 + ox),
            device_id_type=MESH,
        )

    def send_tile(k, carry):
        tile_copy(k, False).start()
        return carry

    def recv_tile(k, carry):
        tile_copy(k, True).wait()
        return carry

    lax.fori_loop(1, 16, send_tile, 0)
    lax.fori_loop(1, 16, recv_tile, 0)

    factor(gt, w)

    mine = 2 * t + h

    def factor_copy(k, landing):
        other = (mine + k) % F
        return pltpu.make_async_remote_copy(
            src_ref=w,
            dst_ref=wa.at[other if landing else mine],
            send_sem=w_ssem.at[other],
            recv_sem=w_rsem.at[other if landing else mine],
            device_id=(other // 2, pair + other % 2),
            device_id_type=MESH,
        )

    def send_factor(k, carry):
        factor_copy(k, False).start()
        return carry

    def recv_factor(k, carry):
        factor_copy(k, True).wait()
        return carry

    lax.fori_loop(1, F, send_factor, 0)
    own_factor = pltpu.make_async_copy(w, wa.at[mine], own_sem)
    own_points.wait()
    own_factor.start()

    def recv_points(k, carry):
        other = (t + k) % NTM
        pltpu.make_async_remote_copy(
            src_ref=spec5.at[other],
            dst_ref=mf.at[:, :, other],
            send_sem=ps_sem.at[other],
            recv_sem=pr_sem.at[other],
            device_id=(other, s),
            device_id_type=MESH,
        ).wait()
        return carry

    lax.fori_loop(1, NTM, recv_points, 0)
    lax.fori_loop(1, F, recv_factor, 0)
    own_factor.wait()


def modes_kernel(w, m, rfac, modes):
    row = lax.broadcasted_iota(jnp.int32, (128, 128), 0)
    col = lax.broadcasted_iota(jnp.int32, (128, 128), 1)
    packed = w[0]
    rfac[0] = jnp.where(col >= row, packed, 0.0)
    inverse = jnp.where(col < row, packed, jnp.where(col == row, 1.0 / packed, 0.0))
    modes[0] = jnp.dot(
        inverse, m[0], preferred_element_type=jnp.float32, precision=lax.Precision.HIGH
    )


def shards(data):
    rows, colsum = make_table()
    f32, bf16 = jnp.float32, jnp.bfloat16
    dma = pltpu.SemaphoreType.DMA
    vmem = pltpu.VMEM
    packed, points = pl.pallas_call(
        main_kernel,
        out_shape=(
            jax.ShapeDtypeStruct((F, 16, 8, 128), f32),
            jax.ShapeDtypeStruct((F, 2, NTM, LB, PTS), f32),
        ),
        in_specs=[
            pl.BlockSpec(memory_space=pl.ANY),
            pl.BlockSpec(memory_space=pltpu.VMEM),
            pl.BlockSpec(memory_space=pltpu.SMEM),
        ],
        out_specs=[pl.BlockSpec(memory_space=pl.ANY), pl.BlockSpec(memory_space=pl.ANY)],
        scratch_shapes=[
            vmem((CHUNKS, NT // NTM, CW), bf16),
            vmem((NTM, 2 * F * LB, PTS), f32),
            vmem((F, 2 * LB, COLS), bf16),
            vmem((2, 2 * NB, COLS), bf16),
            vmem((NTM, 8, 128), f32),
            vmem((2 * NB, COLS), f32),
            vmem((2, 16, 8, 128), f32),
            vmem((NSPACE, 8, 128), f32),
            vmem((16, 8, 128), f32),
            vmem((16, 8, 128), f32),
            dma((CHUNKS,)),
            dma((CHUNKS, NTM)),
            dma((CHUNKS, NTM)),
            dma((NTM,)),
            dma((NTM,)),
            dma((NTM,)),
            dma((NTM,)),
            dma((NSPACE,)),
            dma((NSPACE,)),
            dma((16,)),
            dma((16,)),
            dma((F,)),
            dma((F,)),
            dma,
        ],
        compiler_params=pltpu.CompilerParams(
            collective_id=0, has_side_effects=True, vmem_limit_bytes=32 * 1024 * 1024
        ),
        name="factors",
    )(data, jnp.asarray(rows), jnp.asarray(colsum))
    spec = pl.BlockSpec((1, 128, 128), lambda f: (f, 0, 0))
    return pl.pallas_call(
        modes_kernel,
        grid=(F,),
        out_shape=(
            jax.ShapeDtypeStruct((F, 128, 128), f32),
            jax.ShapeDtypeStruct((F, 128, PTS), f32),
        ),
        in_specs=[spec, spec],
        out_specs=[spec, spec],
        name="modes",
    )(packed.reshape(F, 128, 128), points.reshape(F, 128, PTS))


def solution(mesh):
    return jax.shard_map(
        shards,
        mesh=mesh,
        in_specs=(P("tm", "space"),),
        out_specs=(P(), P(None, None, ("space", "tm"))),
        check_vma=False,
    )
```

time: 696 us -> 71.9 us (0.10)
  other arithmetic: 354 us -> 0 us
  waiting for transfers between devices: 301 us -> 0 us
  Pallas kernels: 0 us -> 64.8 us
  between operations: 14.8 us -> 0.66 us
  matrix products: 9.09 us -> 0 us
  starting transfers between devices: 7.66 us -> 0 us
    another operation x6 -> x0, other arithmetic: 347 us -> none  [the longest x4 188 us: shards(): lower = jnp.linalg.cholesky(gram)]
    psum x1 -> x0, waiting for transfers between devices: 254 us -> none  [shards(): gram = lax.psum(local_gram, ('tm', 'space'))]
    pallas_call x0 -> x2, Pallas kernels: none -> 64.8 us  [the longest x1 54.8 us: shards(): pl.pallas_call(main_kernel, out_shape=(jax.ShapeDtypeStruct((F, 16, 8, 12...]
    all_to_all x1 -> x0, waiting for transfers between devices: 47.3 us -> none  [shards(): lax.all_to_all(cube, 'tm', split_axis=1, concat_axis=0, tiled=True)[:, 0, :]]
    all_to_all x1 -> x0, starting transfers between devices: 7.66 us -> none  [shards(): lax.all_to_all(cube, 'tm', split_axis=1, concat_axis=0, tiled=True)[:, 0, :]]
  transfers between devices with their start and end apart: 2 -> 0, of which waited for: 2 -> 0; matrix products, arithmetic and copies ran while one was open for 0% -> 0% of each run, Pallas kernels for 0% -> 0%
where the time goes in v1:
time: 71.9 us; the launch traced here: 71.1 us
  Pallas kernels  64.8 us (90%)
  local copies, waits for them, and re-layouts  5.56 us (8%)
    pallas_call x1, Pallas kernels, shards(): pl.pallas_call(main_kernel, out_shape=(jax.ShapeDtypeStruct((F, 16, 8, 12...  54.8 us
    pallas_call x1, Pallas kernels, shards(): pl.pallas_call(modes_kernel, grid=(F,), out_shape=(jax.ShapeDtypeStruct((...  10.1 us
    unnamed x10, local copies, waits for them, and re-layouts  5.56 us

profile of v1, /device:TPU:1, one launch (start us, length us, event | category | flops | bytes accessed | tf_op | source)
XLA Modules:
  0.0 71.1 jit_solution(6068804337467445650)
XLA Ops:
  0.6 0.0 copy-start
  0.6 2.2 %copy-done = bf16[2048,1024]{1,0:T(8,128)(2,1)S(1)} copy-done((bf16[2048,1024]{1,0:T(8,128)(2,1)S(1)}, bf16[2048,1024]{1,0:T(8,128)(2,1)}, u32[]{:S(2)}) %copy-start) | copy-done | bytes 4194328
  2.8 0.0 copy-start.3
  2.8 0.7 %copy-done.3 = bf16[48,256]{1,0:T(8,128)(2,1)S(1)} copy-done((bf16[48,256]{1,0:T(8,128)(2,1)S(1)}, bf16[48,256]{1,0:T(8,128)(2,1)}, u32[]{:S(2)}) %copy-start.3) | copy-done | bytes 24600
  3.6 0.0 copy-start.4
  3.6 0.7 copy-done.4
  4.2 54.8 %factors.1 = (f32[16,16,8,128]{3,2,1,0:T(8,128)S(1)}, f32[16,2,8,8,128]{4,3,2,1,0:T(8,128)S(1)}) custom-call(bf16[2048,1024]{1,0:T(8,128)(2,1)S(1)} %copy-done, bf16[48,256]{1,0:T(8,128)(2,1)S(1)} %copy-done.3, f32[32]{0:T(128)S(1)} %copy-done.4), custom_call_target="tpu_custom_call" | custom-call | tf_op jit(solution)/shard_map/factors/pallas_call | solution.py:394
  59.0 0.0 copy-start.1
  59.0 1.0 %copy-done.1 = f32[16,16,8,128]{3,2,1,0:T(8,128)} copy-done((f32[16,16,8,128]{3,2,1,0:T(8,128)}, f32[16,16,8,128]{3,2,1,0:T(8,128)S(1)}, u32[]{:S(2)}) %copy-start.1) | copy-done | bytes 1048600
  59.9 0.0 copy-start.2
  59.9 1.0 %copy-done.2 = f32[16,2,8,8,128]{4,3,2,1,0:T(8,128)} copy-done((f32[16,2,8,8,128]{4,3,2,1,0:T(8,128)}, f32[16,2,8,8,128]{4,3,2,1,0:T(8,128)S(1)}, u32[]{:S(2)}) %copy-start.2) | copy-done | bytes 1048600
  61.0 10.1 %modes.1 = (f32[16,128,128]{2,1,0:T(8,128)}, f32[16,128,128]{2,1,0:T(8,128)}) custom-call(f32[16,128,128]{2,1,0:T(8,128)} %bitcast.2, f32[16,128,128]{2,1,0:T(8,128)} %bitcast.3), custom_call_target="tpu_custom_call" | custom-call | tf_op jit(solution)/shard_map/modes/pallas_call | solution.py:438
Async XLA Ops:
  0.6 2.2 %copy-start = (bf16[2048,1024]{1,0:T(8,128)(2,1)S(1)}, bf16[2048,1024]{1,0:T(8,128)(2,1)}, u32[]{:S(2)}) copy-start(bf16[2048,1024]{1,0:T(8,128)(2,1)} %data.1) | copy-start | bytes 12582916
  2.8 0.7 %copy-start.3 = (bf16[48,256]{1,0:T(8,128)(2,1)S(1)}, bf16[48,256]{1,0:T(8,128)(2,1)}, u32[]{:S(2)}) copy-start(bf16[48,256]{1,0:T(8,128)(2,1)} %constant.4.clone.tab) | copy-start | bytes 73732
  3.6 0.7 copy-start.4
  59.0 1.0 %copy-start.1 = (f32[16,16,8,128]{3,2,1,0:T(8,128)}, f32[16,16,8,128]{3,2,1,0:T(8,128)S(1)}, u32[]{:S(2)}) copy-start(f32[16,16,8,128]{3,2,1,0:T(8,128)S(1)} %get-tuple-element.4) | copy-start | bytes 3145732
  59.9 1.0 %copy-start.2 = (f32[16,2,8,8,128]{4,3,2,1,0:T(8,128)}, f32[16,2,8,8,128]{4,3,2,1,0:T(8,128)S(1)}, u32[]{:S(2)}) copy-start(f32[16,2,8,8,128]{4,3,2,1,0:T(8,128)S(1)} %get-tuple-element.5) | copy-start | bytes 3145732

commit v2 on v1

v2 whole, which is shorter than its diff:
```python
import functools

import jax
import jax.numpy as jnp
import ml_dtypes
import numpy as np
from jax import lax
from jax.experimental import pallas as pl
from jax.experimental.pallas import tpu as pltpu
from jax.sharding import PartitionSpec as P

NFFT = 256
NB = 64
F = 16
NT = 16384
NX = 32768
NTM = 8
NSPACE = 32
LB = NB // NTM
COLS = NX // NSPACE
PTS = COLS // NTM
CHUNKS = 4
CW = COLS // CHUNKS
MESH = pl.DeviceIdType.MESH


def make_table():
    steps = np.arange(NFFT)
    window = 0.5 - 0.5 * np.cos(2.0 * np.pi * steps / NFFT)
    factor = 1.0 / np.sqrt(np.sum(window * window))
    freqs = np.arange(1, F + 1)
    phases = (steps[:, None] * freqs[None, :] % NFFT) * (2.0 * np.pi / NFFT)
    real = np.cos(phases) * (factor * window)[:, None]
    imag = -np.sin(phases) * (factor * window)[:, None]
    pairs = np.stack([real.T, imag.T], axis=1).reshape(2 * F, NFFT)
    rounded = pairs.astype(np.float32).astype(ml_dtypes.bfloat16)
    colsum = rounded.astype(np.float32).sum(axis=1, dtype=np.float32)
    rows = np.zeros((48, NFFT), ml_dtypes.bfloat16)
    rows[: 2 * F] = rounded
    rows[2 * F] = 1.0
    return rows, colsum


def factor(gt_ref, w_ref):
    lane = lax.broadcasted_iota(jnp.int32, (8, 128), 1)
    sub = lax.broadcasted_iota(jnp.int32, (8, 128), 0)
    for j in range(16):
        w_ref[j] = gt_ref[j]
    for k in range(16):
        base = 8 * k
        own = w_ref[k]
        cols = [jnp.broadcast_to(own[:, base + i : base + i + 1], (8, 128)) for i in range(8)]
        pivot_rows, inverses, cross = [], [], []
        diag = jnp.ones((8, 128), jnp.float32)
        for i in range(8):
            d = jnp.broadcast_to(cols[i][i : i + 1, :], (8, 128))
            inv = 1.0 / d
            row = jnp.broadcast_to(own[i : i + 1, :], (8, 128))
            diag = jnp.where(sub == i, d, diag)
            f = jnp.where(sub > i, cols[i] * inv, 0.0)
            here = [jnp.broadcast_to(cols[m][i : i + 1, :], (8, 128)) for m in range(i + 1, 8)]
            for n, m in enumerate(range(i + 1, 8)):
                cols[m] = cols[m] - f * here[n]
            unit = jnp.where(lane == base + i, 1.0, row)
            own = jnp.where((lane == base + i) & (sub > i), 0.0, own) - f * unit
            pivot_rows.append(jnp.where((lane > base + i) & (lane < base + 8), 0.0, unit))
            inverses.append(inv)
            cross.append(here)
        w_ref[k] = own * lax.rsqrt(diag)
        for j in range(k + 1, 16):
            rest = w_ref[j]
            mult = [jnp.broadcast_to(rest[:, base + i : base + i + 1], (8, 128)) for i in range(8)]
            rest = jnp.where((lane >= base) & (lane < base + 8), 0.0, rest)
            for i in range(8):
                f = mult[i] * inverses[i]
                for n, m in enumerate(range(i + 1, 8)):
                    mult[m] = mult[m] - f * cross[i][n]
                rest = rest - f * pivot_rows[i]
            w_ref[j] = rest


def plane_distance(dz, dx):
    return min(dz, 8 - dz) + min(dx, 4 - dx)


PLANE = sorted(
    [(dz, dx) for dz in range(8) for dx in range(4) if dz or dx],
    key=lambda o: -plane_distance(*o),
)
HALF = [o for o in PLANE if o[1] % 2 == 0]
GROUP = [(2, 0), (2, 1), (1, 0), (3, 0), (1, 1), (3, 1), (0, 1)]
SHARE = [(2, 1), (2, 0), (1, 1), (3, 1), (1, 0), (3, 0), (0, 1)]


def main_kernel(
    colsum,
    data, tab_hbm, rfac, modes,
    tab, cs, dbuf, spec, sb, rb, ls, mat, gs, gr, gt, w, wa, mf,
    tab_sem, load_sem, fs_sem, fr_sem, ls_ssem, ls_rsem, ps_sem, pr_sem,
    ga_ssem, ga_rsem, gb_ssem, gb_rsem, w_ssem, w_rsem, r_ssem, r_rsem, own_sem,
):
    t = lax.axis_index("tm")
    s = lax.axis_index("space")
    y, core = t // 2, t % 2
    z, x = s // 4, s % 4
    h = x % 2
    tile = (x // 2) * 8 + z
    pair = z * 4 + (x // 2) * 2
    sibling = 2 * y + 1 - core

    load_tab = pltpu.make_async_copy(tab_hbm, tab, tab_sem)
    load_tab.start()
    loads = []
    for c in range(CHUNKS):
        copy = pltpu.make_async_copy(
            data.at[:, pl.ds(c * CW, CW)], dbuf.at[c], load_sem.at[c]
        )
        copy.start()
        loads.append(copy)

    def remote(src, dst, send_sem, recv_sem, device):
        return pltpu.make_async_remote_copy(
            src_ref=src,
            dst_ref=dst,
            send_sem=send_sem,
            recv_sem=recv_sem,
            device_id=device,
            device_id_type=MESH,
        )

    def group_peer(o):
        return ((y + o[0]) % 4) * 2 + (core + o[1]) % 2

    def group_source(o):
        return ((y + 4 - o[0]) % 4) * 2 + (core + o[1]) % 2

    def plane_peer(o):
        return ((z + o[0]) % 8) * 4 + (x + o[1]) % 4

    barrier = pltpu.get_barrier_semaphore()
    for o in PLANE:
        pl.semaphore_signal(barrier, inc=1, device_id=(t, plane_peer(o)), device_id_type=MESH)
    for o in GROUP:
        pl.semaphore_signal(barrier, inc=1, device_id=(group_peer(o), s), device_id_type=MESH)
    for o in GROUP:
        pl.semaphore_signal(
            barrier, inc=1, device_id=(group_peer(o), pair + 1 - h), device_id_type=MESH
        )

    for j in range(2 * F):
        cs[j] = jnp.float32(colsum[j])
    load_tab.wait()
    table = tab[...].astype(jnp.bfloat16)
    sends = []

    for c in range(CHUNKS):
        cols = pl.ds(c * CW, CW)
        loads[c].wait()
        total = jnp.zeros((1, CW), jnp.float32)
        for b in range(LB):
            out = jnp.dot(
                table, dbuf[c, pl.ds(b * NFFT, NFFT), :], preferred_element_type=jnp.float32
            )
            for r in range(CW // 128):
                spec[c * (CW // 128) + r, pl.ds(b, 2 * F, stride=LB), :] = out[
                    : 2 * F, r * 128 : (r + 1) * 128
                ]
            total = total + out[2 * F : 2 * F + 1]
        for r in range(CW // 128):
            ls[t, pl.ds(c * (CW // 128) + r, 1), :] = total[:, r * 128 : (r + 1) * 128]
        local_mean = jnp.broadcast_to(total * (NTM / NT), (LB, CW))
        for r in range(CW // 128):
            place = c * (CW // 128) + r
            for f in range(F):
                parts = [
                    spec[place, pl.ds(f * 16 + ri * 8, 8), :]
                    - colsum[2 * f + ri] * local_mean[:, r * 128 : (r + 1) * 128]
                    for ri in range(2)
                ]
                sb[f, :, pl.ds(place * 128, 128)] = jnp.concatenate(parts, axis=0).astype(
                    jnp.bfloat16
                )
        if c == 0:
            pl.semaphore_wait(barrier, 2 * len(GROUP) + len(PLANE))
        for i, o in enumerate(GROUP):
            other = group_peer(o)
            copy = remote(
                sb.at[pl.ds(2 * other, 2), :, cols],
                rb.at[:, pl.ds(pl.multiple_of(t * 16, 16), 16), cols],
                fs_sem.at[c, i],
                fr_sem.at[c, i],
                (other, s),
            )
            copy.start()
            sends.append(copy)

    for i, o in enumerate(GROUP):
        copy = remote(ls.at[t], ls.at[t], ls_ssem.at[i], ls_rsem.at[i], (group_peer(o), s))
        copy.start()
        sends.append(copy)
    for f2 in range(2):
        rb[f2, pl.ds(pl.multiple_of(t * 16, 16), 16), :] = sb[2 * t + f2]

    for i, o in enumerate(GROUP):
        source = group_source(o)
        remote(
            ls.at[t], ls.at[source], ls_ssem.at[i], ls_rsem.at[i], (source, s)
        ).wait_recv()
    mean = ls[0]
    for k in range(1, NTM):
        mean = mean + ls[k]
    mean = mean * (1.0 / NT)

    def subtract(f, carry):
        for ri in range(2):
            rows = pl.ds(pl.multiple_of(f * 16 + ri * 8, 8), 8)
            for r in range(8):
                spec[r, rows, :] = spec[r, rows, :] - cs[2 * f + ri] * mean[r : r + 1, :]
        return carry

    lax.fori_loop(0, F, subtract, 0)
    spec5 = spec.reshape(NTM, F, 2, LB, PTS)
    for i, o in enumerate(GROUP):
        other = group_peer(o)
        copy = remote(spec5.at[other], mf.at[:, :, t], ps_sem.at[i], pr_sem.at[i], (other, s))
        copy.start()
        sends.append(copy)
    own_points = pltpu.make_async_copy(spec5.at[t], mf.at[:, :, t], own_sem)
    own_points.start()

    for i, o in enumerate(GROUP):
        source = group_source(o)
        for c in range(CHUNKS):
            cols = pl.ds(c * CW, CW)
            remote(
                sb.at[pl.ds(2 * source, 2), :, cols],
                rb.at[:, pl.ds(pl.multiple_of(source * 16, 16), 16), cols],
                fs_sem.at[c, i],
                fr_sem.at[c, i],
                (source, s),
            ).wait_recv()
    for f2 in range(2):
        real, imag = cs[4 * t + 2 * f2], cs[4 * t + 2 * f2 + 1]

        def gather(k, carry):
            shift = ls[k] * (NTM / NT) - mean
            for r in range(8):
                lanes = pl.ds(r * 128, 128)
                block = rb[f2, pl.ds(pl.multiple_of(k * 16, 16), 16), lanes].astype(jnp.float32)
                row = jnp.broadcast_to(shift[r : r + 1, :], (8, 128))
                mat[pl.ds(pl.multiple_of(k * 8, 8), 8), lanes] = block[:8] + real * row
                mat[pl.ds(pl.multiple_of(64 + k * 8, 8), 8), lanes] = block[8:] + imag * row
            return carry

        lax.fori_loop(0, NTM, gather, 0)
        rounded = mat[...].astype(jnp.bfloat16)
        gram = lax.dot_general(
            rounded, rounded, (((1,), (1,)), ((), ())), preferred_element_type=jnp.float32
        ) * (1.0 / NX)
        for i in range(16):
            gs[f2, i] = gram[i * 8 : (i + 1) * 8]

    for i, o in enumerate(PLANE):
        oz, ox = (z + o[0]) % 8, (x + o[1]) % 4
        copy = remote(
            gs.at[ox % 2, (ox // 2) * 8 + oz],
            gr.at[i],
            ga_ssem.at[i],
            ga_rsem.at[i],
            (t, oz * 4 + ox),
        )
        copy.start()
        sends.append(copy)
    rows = gs[h, tile]
    for i in reversed(range(len(PLANE))):
        remote(gs.at[0, 0], gr.at[i], ga_ssem.at[i], ga_rsem.at[i], (t, s)).wait_recv()
        rows = rows + gr[i]
    gt[tile] = rows

    for i, o in enumerate(HALF):
        copy = remote(
            gt.at[tile], gt.at[tile], gb_ssem.at[i], gb_rsem.at[i], (t, plane_peer(o))
        )
        copy.start()
        sends.append(copy)
    for i, o in enumerate(HALF):
        oz, ox = (z + 8 - o[0]) % 8, (x + o[1]) % 4
        source = (ox // 2) * 8 + oz
        remote(
            gt.at[tile], gt.at[source], gb_ssem.at[i], gb_rsem.at[i], (t, oz * 4 + ox)
        ).wait_recv()

    factor(gt, w)

    mine = 2 * t + h
    for i, o in enumerate(SHARE):
        peer = (((y + o[0]) % 4) * 2 + core, pair + (h + o[1]) % 2)
        copy = remote(w, wa.at[mine], w_ssem.at[i], w_rsem.at[i], peer)
        copy.start()
        sends.append(copy)
    copy = remote(w, wa.at[mine], r_ssem.at[7], r_rsem.at[7], (sibling, s))
    copy.start()
    sends.append(copy)
    own_points.wait()
    for i, o in enumerate(GROUP):
        source = group_source(o)
        remote(
            spec5.at[source], mf.at[:, :, source], ps_sem.at[i], pr_sem.at[i], (source, s)
        ).wait_recv()
    row = lax.broadcasted_iota(jnp.int32, (128, 128), 0)
    col = lax.broadcasted_iota(jnp.int32, (128, 128), 1)

    def multiply(f, packed):
        packed = packed.reshape(128, 128)
        rfac[f] = jnp.where(col >= row, packed, 0.0)
        inverse = jnp.where(col < row, packed, jnp.where(col == row, 1.0 / packed, 0.0))
        modes[f] = jnp.dot(
            inverse,
            mf[f].reshape(128, PTS),
            preferred_element_type=jnp.float32,
            precision=lax.Precision.HIGH,
        )

    multiply(mine, w[...])
    for i in reversed(range(len(SHARE))):
        o = SHARE[i]
        f = 4 * ((y + 4 - o[0]) % 4) + 2 * core + (h + o[1]) % 2
        remote(w, wa.at[f], w_ssem.at[i], w_rsem.at[i], (sibling, s)).wait_recv()
        copy = remote(wa.at[f], wa.at[f], r_ssem.at[i], r_rsem.at[i], (sibling, s))
        copy.start()
        sends.append(copy)
        multiply(f, wa[f])
    for i in reversed(range(len(SHARE) + 1)):
        o = SHARE[i] if i < len(SHARE) else (0, 0)
        f = 4 * ((y + 4 - o[0]) % 4) + 2 * (1 - core) + (h + o[1]) % 2
        remote(w, wa.at[f], r_ssem.at[i], r_rsem.at[i], (sibling, s)).wait_recv()
        multiply(f, wa[f])
    for copy in sends:
        copy.wait_send()


def hand_out(rfac, modes, rfac_out, modes_out, sems):
    copies = [
        pltpu.make_async_copy(rfac, rfac_out, sems.at[0]),
        pltpu.make_async_copy(modes, modes_out, sems.at[1]),
    ]
    for copy in copies:
        copy.start()
    for copy in copies:
        copy.wait()


def shards(data):
    rows, colsum = make_table()
    f32, bf16 = jnp.float32, jnp.bfloat16
    dma = pltpu.SemaphoreType.DMA
    vmem = pltpu.VMEM
    rfac, modes = pl.pallas_call(
        functools.partial(main_kernel, [float(v) for v in colsum]),
        out_shape=(vmem((F, 128, 128), f32), vmem((F, 128, PTS), f32)),
        in_specs=[pl.BlockSpec(memory_space=pltpu.HBM), pl.BlockSpec(memory_space=pltpu.HBM)],
        out_specs=[pl.BlockSpec(memory_space=pltpu.VMEM), pl.BlockSpec(memory_space=pltpu.VMEM)],
        scratch_shapes=[
            vmem((48, NFFT), f32),
            pltpu.SMEM((2 * F,), f32),
            vmem((CHUNKS, NT // NTM, CW), bf16),
            vmem((NTM, 2 * F * LB, PTS), f32),
            vmem((F, 2 * LB, COLS), bf16),
            vmem((2, 2 * NB, COLS), bf16),
            vmem((NTM, 8, 128), f32),
            vmem((2 * NB, COLS), f32),
            vmem((2, 16, 8, 128), f32),
            vmem((NSPACE, 8, 128), f32),
            vmem((16, 8, 128), f32),
            vmem((16, 8, 128), f32),
            vmem((F, 16, 8, 128), f32),
            vmem((F, 2, NTM, LB, PTS), f32),
            dma,
            dma((CHUNKS,)),
            dma((CHUNKS, 7)),
            dma((CHUNKS, 7)),
            dma((7,)),
            dma((7,)),
            dma((7,)),
            dma((7,)),
            dma((NSPACE,)),
            dma((NSPACE,)),
            dma((16,)),
            dma((16,)),
            dma((7,)),
            dma((7,)),
            dma((8,)),
            dma((8,)),
            dma,
        ],
        compiler_params=pltpu.CompilerParams(
            collective_id=0, has_side_effects=True, vmem_limit_bytes=56 * 1024 * 1024
        ),
        name="factors",
    )(data, jnp.asarray(rows.astype(np.float32)))
    return pl.pallas_call(
        hand_out,
        out_shape=(
            jax.ShapeDtypeStruct((F, 128, 128), f32),
            jax.ShapeDtypeStruct((F, 128, PTS), f32),
        ),
        in_specs=[pl.BlockSpec(memory_space=pltpu.VMEM), pl.BlockSpec(memory_space=pltpu.VMEM)],
        out_specs=[pl.BlockSpec(memory_space=pl.ANY), pl.BlockSpec(memory_space=pl.ANY)],
        scratch_shapes=[dma((2,))],
        compiler_params=pltpu.CompilerParams(vmem_limit_bytes=8 * 1024 * 1024),
        name="hand_out",
    )(rfac, modes)


def solution(mesh):
    return jax.shard_map(
        shards,
        mesh=mesh,
        in_specs=(P("tm", "space"),),
        out_specs=(P(), P(None, None, ("space", "tm"))),
        check_vma=False,
    )
```

time: 71.9 us -> 50.1 us (0.70); the launches traced: 71.1 us -> 50 us
  Pallas kernels: 64.8 us -> 49.4 us
  local copies, waits for them, and re-layouts: 5.56 us -> 0 us
    pallas_call x2, Pallas kernels: 64.8 us -> 49.4 us  [the longest x1 48 us: shards(): pl.pallas_call(functools.partial(main_kernel, [float(v) for v in colsum])...]
    unnamed x10 -> x0, local copies, waits for them, and re-layouts: 5.56 us -> none
where the time goes in v2:
time: 50.1 us; the launch traced here: 50 us
  Pallas kernels  49.4 us (99%)
  between operations  0.64 us (1%)
    pallas_call x1, Pallas kernels, shards(): pl.pallas_call(functools.partial(main_kernel, [float(v) for v in colsum])...  48 us
    pallas_call x1, Pallas kernels, shards(): pl.pallas_call(hand_out, out_shape=(jax.ShapeDtypeStruct((F, 128, 128), f...  1.33 us

profile of v2, /device:TPU:1, one launch (start us, length us, event | category | flops | bytes accessed | tf_op | source)
XLA Modules:
  0.0 50.0 jit_solution(3238770519539126694)
XLA Ops:
  0.6 48.0 %factors.1 = (f32[16,128,128]{2,1,0:T(8,128)S(1)}, f32[16,128,128]{2,1,0:T(8,128)S(1)}) custom-call(bf16[2048,1024]{1,0:T(8,128)(2,1)} %data.1, f32[48,256]{1,0:T(8,128)} %constant.2.clone.tab_hbm), custom_call_target="tpu_custom_call" | custom-call | tf_op jit(solution)/shard_map/factors/pallas_call | solution.py:358
  48.7 1.3 %hand_out.1 = (f32[16,128,128]{2,1,0:T(8,128)}, f32[16,128,128]{2,1,0:T(8,128)}) custom-call(f32[16,128,128]{2,1,0:T(8,128)S(1)} %get-tuple-element.4.rfac, f32[16,128,128]{2,1,0:T(8,128)S(1)} %get-tuple-element.5.modes), custom_call_target="tpu_custom_call" | custom-call | tf_op jit(solution)/shard_map/hand_out/pallas_call | solution.py:401

commit v3 on v2

--- a/solution.py
+++ b/solution.py
@@ -87,9 +87,10 @@
     [(dz, dx) for dz in range(8) for dx in range(4) if dz or dx],
     key=lambda o: -plane_distance(*o),
 )
-HALF = [o for o in PLANE if o[1] % 2 == 0]
+OFFSET_Y = (1, 3, 2, 0, 1, 3, 2)
+HALF = [o for o in PLANE if sum(o) % 2 == 0]
+OTHER = [o for o in PLANE if sum(o) % 2 == 1]
 GROUP = [(2, 0), (2, 1), (1, 0), (3, 0), (1, 1), (3, 1), (0, 1)]
-SHARE = [(2, 1), (2, 0), (1, 1), (3, 1), (1, 0), (3, 0), (0, 1)]
 
 
 def main_kernel(
@@ -98,14 +99,14 @@
     tab, cs, dbuf, spec, sb, rb, ls, mat, gs, gr, gt, w, wa, mf,
     tab_sem, load_sem, fs_sem, fr_sem, ls_ssem, ls_rsem, ps_sem, pr_sem,
     ga_ssem, ga_rsem, gb_ssem, gb_rsem, w_ssem, w_rsem, r_ssem, r_rsem, own_sem,
+    group_in, plane_in,
 ):
     t = lax.axis_index("tm")
     s = lax.axis_index("space")
     y, core = t // 2, t % 2
     z, x = s // 4, s % 4
-    h = x % 2
-    tile = (x // 2) * 8 + z
-    pair = z * 4 + (x // 2) * 2
+    h = (x + z) % 2
+    tile = z * 2 + x // 2
     sibling = 2 * y + 1 - core
 
     load_tab = pltpu.make_async_copy(tab_hbm, tab, tab_sem)
@@ -138,14 +139,20 @@
         return ((z + o[0]) % 8) * 4 + (x + o[1]) % 4
 
     barrier = pltpu.get_barrier_semaphore()
-    for o in PLANE:
-        pl.semaphore_signal(barrier, inc=1, device_id=(t, plane_peer(o)), device_id_type=MESH)
-    for o in GROUP:
-        pl.semaphore_signal(barrier, inc=1, device_id=(group_peer(o), s), device_id_type=MESH)
-    for o in GROUP:
-        pl.semaphore_signal(
-            barrier, inc=1, device_id=(group_peer(o), pair + 1 - h), device_id_type=MESH
-        )
+
+    def signal(sem, device):
+        pl.semaphore_signal(sem, inc=1, device_id=device, device_id_type=MESH)
+
+    for dy in range(4):
+        other = ((y + dy) % 4) * 2
+        if dy == 0:
+
+            @pl.when(core == 1)
+            def _():
+                signal(barrier, (other, s))
+
+        else:
+            signal(barrier, (other, s))
 
     for j in range(2 * F):
         cs[j] = jnp.float32(colsum[j])
@@ -180,24 +187,38 @@
                 sb[f, :, pl.ds(place * 128, 128)] = jnp.concatenate(parts, axis=0).astype(
                     jnp.bfloat16
                 )
-        if c == 0:
-            pl.semaphore_wait(barrier, 2 * len(GROUP) + len(PLANE))
+
+    @pl.when(core == 0)
+    def _():
+        pl.semaphore_wait(barrier, len(GROUP))
+        signal(group_in, (sibling, s))
+
+    @pl.when(core == 1)
+    def _():
+        pl.semaphore_wait(group_in, 1)
+
+    for i, o in enumerate(GROUP):
+        copy = remote(ls.at[t], ls.at[t], ls_ssem.at[i], ls_rsem.at[i], (group_peer(o), s))
+        copy.start()
+        sends.append(copy)
+    for f2 in range(2):
         for i, o in enumerate(GROUP):
             other = group_peer(o)
             copy = remote(
-                sb.at[pl.ds(2 * other, 2), :, cols],
-                rb.at[:, pl.ds(pl.multiple_of(t * 16, 16), 16), cols],
-                fs_sem.at[c, i],
-                fr_sem.at[c, i],
+                sb.at[2 * other + f2],
+                rb.at[f2, pl.ds(pl.multiple_of(t * 16, 16), 16), :],
+                fs_sem.at[f2, i],
+                fr_sem.at[f2, i],
                 (other, s),
             )
             copy.start()
             sends.append(copy)
 
-    for i, o in enumerate(GROUP):
-        copy = remote(ls.at[t], ls.at[t], ls_ssem.at[i], ls_rsem.at[i], (group_peer(o), s))
-        copy.start()
-        sends.append(copy)
+    @pl.when(core == 1)
+    def _():
+        for o in PLANE:
+            signal(barrier, (t, plane_peer(o)))
+
     for f2 in range(2):
         rb[f2, pl.ds(pl.multiple_of(t * 16, 16), 16), :] = sb[2 * t + f2]
 
@@ -220,26 +241,17 @@
 
     lax.fori_loop(0, F, subtract, 0)
     spec5 = spec.reshape(NTM, F, 2, LB, PTS)
-    for i, o in enumerate(GROUP):
-        other = group_peer(o)
-        copy = remote(spec5.at[other], mf.at[:, :, t], ps_sem.at[i], pr_sem.at[i], (other, s))
-        copy.start()
-        sends.append(copy)
-    own_points = pltpu.make_async_copy(spec5.at[t], mf.at[:, :, t], own_sem)
-    own_points.start()
-
-    for i, o in enumerate(GROUP):
-        source = group_source(o)
-        for c in range(CHUNKS):
-            cols = pl.ds(c * CW, CW)
+
+    for f2 in range(2):
+        for i, o in enumerate(GROUP):
+            source = group_source(o)
             remote(
-                sb.at[pl.ds(2 * source, 2), :, cols],
-                rb.at[:, pl.ds(pl.multiple_of(source * 16, 16), 16), cols],
-                fs_sem.at[c, i],
-                fr_sem.at[c, i],
+                sb.at[source],
+                rb.at[f2, pl.ds(pl.multiple_of(source * 16, 16), 16), :],
+                fs_sem.at[f2, i],
+                fr_sem.at[f2, i],
                 (source, s),
             ).wait_recv()
-    for f2 in range(2):
         real, imag = cs[4 * t + 2 * f2], cs[4 * t + 2 * f2 + 1]
 
         def gather(k, carry):
@@ -260,17 +272,53 @@
         for i in range(16):
             gs[f2, i] = gram[i * 8 : (i + 1) * 8]
 
-    for i, o in enumerate(PLANE):
-        oz, ox = (z + o[0]) % 8, (x + o[1]) % 4
-        copy = remote(
-            gs.at[ox % 2, (ox // 2) * 8 + oz],
-            gr.at[i],
-            ga_ssem.at[i],
-            ga_rsem.at[i],
-            (t, oz * 4 + ox),
-        )
-        copy.start()
-        sends.append(copy)
+        if f2 == 0:
+
+            @pl.when(core == 1)
+            def _():
+                pl.semaphore_wait(barrier, len(PLANE))
+                signal(plane_in, (sibling, s))
+
+            @pl.when(core == 0)
+            def _():
+                pl.semaphore_wait(plane_in, 1)
+
+        change = (h + f2) % 2
+
+        def choose(a, b):
+            return jnp.where(change == 0, a, b)
+
+        def send_rows(i):
+            keep = HALF[min(i, len(HALF) - 1)]
+            oz = (z + choose(keep[0], OTHER[i][0])) % 8
+            ox = (x + choose(keep[1], OTHER[i][1])) % 4
+            k = choose(PLANE.index(keep), PLANE.index(OTHER[i]))
+            remote(
+                gs.at[f2, oz * 2 + ox // 2],
+                gr.at[k],
+                ga_ssem.at[k],
+                ga_rsem.at[k],
+                (t, oz * 4 + ox),
+            ).start()
+
+        for i in range(len(HALF)):
+            send_rows(i)
+
+        @pl.when(change == 1)
+        def _():
+            send_rows(len(HALF))
+
+        if f2 == 0:
+            for i, o in enumerate(GROUP):
+                other = group_peer(o)
+                copy = remote(
+                    spec5.at[other], mf.at[:, :, t], ps_sem.at[i], pr_sem.at[i], (other, s)
+                )
+                copy.start()
+                sends.append(copy)
+            own_points = pltpu.make_async_copy(spec5.at[t], mf.at[:, :, t], own_sem)
+            own_points.start()
+
     rows = gs[h, tile]
     for i in reversed(range(len(PLANE))):
         remote(gs.at[0, 0], gr.at[i], ga_ssem.at[i], ga_rsem.at[i], (t, s)).wait_recv()
@@ -284,8 +332,8 @@
         copy.start()
         sends.append(copy)
     for i, o in enumerate(HALF):
-        oz, ox = (z + 8 - o[0]) % 8, (x + o[1]) % 4
-        source = (ox // 2) * 8 + oz
+        oz, ox = (z + 8 - o[0]) % 8, (x + 4 - o[1]) % 4
+        source = oz * 2 + ox // 2
         remote(
             gt.at[tile], gt.at[source], gb_ssem.at[i], gb_rsem.at[i], (t, oz * 4 + ox)
         ).wait_recv()
@@ -293,9 +341,19 @@
     factor(gt, w)
 
     mine = 2 * t + h
-    for i, o in enumerate(SHARE):
-        peer = (((y + o[0]) % 4) * 2 + core, pair + (h + o[1]) % 2)
-        copy = remote(w, wa.at[mine], w_ssem.at[i], w_rsem.at[i], peer)
+    for slot in (2, 6, 5, 4, 1, 0, 3):
+        dy = OFFSET_Y[slot]
+        other_y = (y + dy) % 4
+        if slot < 3:
+            column = s
+        else:
+            d = (y + other_y) % 4
+            dx = jnp.where(d == 0, 1, jnp.where(d == 1, 3, 0))
+            dz = jnp.where(d == 2, 1, jnp.where(d == 3, 7, 0))
+            column = ((z + dz) % 8) * 4 + (x + dx) % 4
+        copy = remote(
+            w, wa.at[mine], w_ssem.at[slot], w_rsem.at[slot], (other_y * 2 + core, column)
+        )
         copy.start()
         sends.append(copy)
     copy = remote(w, wa.at[mine], r_ssem.at[7], r_rsem.at[7], (sibling, s))
@@ -322,19 +380,32 @@
         )
 
     multiply(mine, w[...])
-    for i in reversed(range(len(SHARE))):
-        o = SHARE[i]
-        f = 4 * ((y + 4 - o[0]) % 4) + 2 * core + (h + o[1]) % 2
-        remote(w, wa.at[f], w_ssem.at[i], w_rsem.at[i], (sibling, s)).wait_recv()
-        copy = remote(wa.at[f], wa.at[f], r_ssem.at[i], r_rsem.at[i], (sibling, s))
+    order = [(i + 3 * h) % 7 for i in range(7)]
+
+    def frequency(slot, of_core):
+        turn = slot % 7
+        dy = jnp.where(
+            turn < 3,
+            jnp.where(turn == 2, 2, 1 + 2 * turn),
+            jnp.where(turn == 6, 2, jnp.where(turn == 5, 3, turn - 3)),
+        )
+        half = jnp.where(turn < 3, h, 1 - h)
+        return 4 * ((y + 4 - dy) % 4) + 2 * of_core + half
+
+    for slot in order:
+        f = frequency(slot, core)
+        remote(w, wa.at[f], w_ssem.at[slot], w_rsem.at[slot], (sibling, s)).wait_recv()
+        copy = remote(wa.at[f], wa.at[f], r_ssem.at[slot], r_rsem.at[slot], (sibling, s))
         copy.start()
         sends.append(copy)
         multiply(f, wa[f])
-    for i in reversed(range(len(SHARE) + 1)):
-        o = SHARE[i] if i < len(SHARE) else (0, 0)
-        f = 4 * ((y + 4 - o[0]) % 4) + 2 * (1 - core) + (h + o[1]) % 2
-        remote(w, wa.at[f], r_ssem.at[i], r_rsem.at[i], (sibling, s)).wait_recv()
+    for i in range(8):
+        slot = order[i - 1] if i else 7
+        f = frequency(slot, 1 - core) if i else 4 * y + 2 * (1 - core) + h
+        remote(w, wa.at[f], r_ssem.at[slot], r_rsem.at[slot], (sibling, s)).wait_recv()
         multiply(f, wa[f])
+    for k in range(len(PLANE)):
+        remote(gs.at[0, 0], gr.at[k], ga_ssem.at[k], ga_rsem.at[k], (t, s)).wait_send()
     for copy in sends:
         copy.wait_send()
 
@@ -377,8 +448,8 @@
             vmem((F, 2, NTM, LB, PTS), f32),
             dma,
             dma((CHUNKS,)),
-            dma((CHUNKS, 7)),
-            dma((CHUNKS, 7)),
+            dma((2, 7)),
+            dma((2, 7)),
             dma((7,)),
             dma((7,)),
             dma((7,)),
@@ -392,6 +463,8 @@
             dma((8,)),
             dma((8,)),
             dma,
+            pltpu.SemaphoreType.REGULAR,
+            pltpu.SemaphoreType.REGULAR,
         ],
         compiler_params=pltpu.CompilerParams(
             collective_id=0, has_side_effects=True, vmem_limit_bytes=56 * 1024 * 1024

time: 50.1 us -> 45.9 us (0.916)
  Pallas kernels: 49.4 us -> 45.2 us
    pallas_call x1, Pallas kernels: 48 us -> 43.8 us  [shards(): pl.pallas_call(functools.partial(main_kernel, [float(v) for v in colsum])...]
where the time goes in v3:
time: 45.9 us; the launch traced here: 45.8 us
  Pallas kernels  45.2 us (98%)
  between operations  0.64 us (1%)
    pallas_call x1, Pallas kernels, shards(): pl.pallas_call(functools.partial(main_kernel, [float(v) for v in colsum])...  43.8 us
    pallas_call x1, Pallas kernels, shards(): pl.pallas_call(hand_out, out_shape=(jax.ShapeDtypeStruct((F, 128, 128), f...  1.33 us

profile of v3, /device:TPU:1, one launch (start us, length us, event | category | flops | bytes accessed | tf_op | source)
XLA Modules:
  0.0 45.8 jit_solution(10574564636819515162)
XLA Ops:
  0.6 43.8 %factors.1 = (f32[16,128,128]{2,1,0:T(8,128)S(1)}, f32[16,128,128]{2,1,0:T(8,128)S(1)}) custom-call(bf16[2048,1024]{1,0:T(8,128)(2,1)} %data.1, f32[48,256]{1,0:T(8,128)} %constant.2.clone.tab_hbm), custom_call_target="tpu_custom_call" | custom-call | tf_op jit(solution)/shard_map/factors/pallas_call | solution.py:429
  44.5 1.3 %hand_out.1 = (f32[16,128,128]{2,1,0:T(8,128)}, f32[16,128,128]{2,1,0:T(8,128)}) custom-call(f32[16,128,128]{2,1,0:T(8,128)S(1)} %get-tuple-element.4.rfac, f32[16,128,128]{2,1,0:T(8,128)S(1)} %get-tuple-element.5.modes), custom_call_target="tpu_custom_call" | custom-call | tf_op jit(solution)/shard_map/hand_out/pallas_call | solution.py:474

commit v4 on v3

--- a/solution.py
+++ b/solution.py
@@ -41,7 +41,7 @@
     return rows, colsum
 
 
-def factor(gt_ref, w_ref):
+def factor(gt_ref, w_ref, half_done):
     lane = lax.broadcasted_iota(jnp.int32, (8, 128), 1)
     sub = lax.broadcasted_iota(jnp.int32, (8, 128), 0)
     for j in range(16):
@@ -57,16 +57,20 @@
             inv = 1.0 / d
             row = jnp.broadcast_to(own[i : i + 1, :], (8, 128))
             diag = jnp.where(sub == i, d, diag)
-            f = jnp.where(sub > i, cols[i] * inv, 0.0)
+            f = cols[i] * inv
             here = [jnp.broadcast_to(cols[m][i : i + 1, :], (8, 128)) for m in range(i + 1, 8)]
             for n, m in enumerate(range(i + 1, 8)):
                 cols[m] = cols[m] - f * here[n]
             unit = jnp.where(lane == base + i, 1.0, row)
-            own = jnp.where((lane == base + i) & (sub > i), 0.0, own) - f * unit
+            own = jnp.where((lane == base + i) & (sub > i), 0.0, own) - jnp.where(
+                sub > i, f, 0.0
+            ) * unit
             pivot_rows.append(jnp.where((lane > base + i) & (lane < base + 8), 0.0, unit))
             inverses.append(inv)
             cross.append(here)
         w_ref[k] = own * lax.rsqrt(diag)
+        if k == 7:
+            half_done()
         for j in range(k + 1, 16):
             rest = w_ref[j]
             mult = [jnp.broadcast_to(rest[:, base + i : base + i + 1], (8, 128)) for i in range(8)]
@@ -97,9 +101,8 @@
     colsum,
     data, tab_hbm, rfac, modes,
     tab, cs, dbuf, spec, sb, rb, ls, mat, gs, gr, gt, w, wa, mf,
-    tab_sem, load_sem, fs_sem, fr_sem, ls_ssem, ls_rsem, ps_sem, pr_sem,
-    ga_ssem, ga_rsem, gb_ssem, gb_rsem, w_ssem, w_rsem, r_ssem, r_rsem, own_sem,
-    group_in, plane_in,
+    tab_sem, load_sem, fs_sem, ls_sem, ps_sem, ga_sem, gb_sem,
+    w_ssem, w_rsem, r_ssem, r_rsem, own_sem, group_in, plane_in,
 ):
     t = lax.axis_index("tm")
     s = lax.axis_index("space")
@@ -158,7 +161,6 @@
         cs[j] = jnp.float32(colsum[j])
     load_tab.wait()
     table = tab[...].astype(jnp.bfloat16)
-    sends = []
 
     for c in range(CHUNKS):
         cols = pl.ds(c * CW, CW)
@@ -197,22 +199,21 @@
     def _():
         pl.semaphore_wait(group_in, 1)
 
-    for i, o in enumerate(GROUP):
-        copy = remote(ls.at[t], ls.at[t], ls_ssem.at[i], ls_rsem.at[i], (group_peer(o), s))
-        copy.start()
-        sends.append(copy)
+    def all_of(ref, send_sem, recv_sem):
+        return remote(ref, ref, send_sem, recv_sem, (sibling, s))
+
+    for o in GROUP:
+        remote(ls.at[t], ls.at[t], ls_sem.at[0], ls_sem.at[1], (group_peer(o), s)).start()
     for f2 in range(2):
-        for i, o in enumerate(GROUP):
+        for o in GROUP:
             other = group_peer(o)
-            copy = remote(
+            remote(
                 sb.at[2 * other + f2],
                 rb.at[f2, pl.ds(pl.multiple_of(t * 16, 16), 16), :],
-                fs_sem.at[f2, i],
-                fr_sem.at[f2, i],
+                fs_sem.at[0],
+                fs_sem.at[1 + f2],
                 (other, s),
-            )
-            copy.start()
-            sends.append(copy)
+            ).start()
 
     @pl.when(core == 1)
     def _():
@@ -222,11 +223,8 @@
     for f2 in range(2):
         rb[f2, pl.ds(pl.multiple_of(t * 16, 16), 16), :] = sb[2 * t + f2]
 
-    for i, o in enumerate(GROUP):
-        source = group_source(o)
-        remote(
-            ls.at[t], ls.at[source], ls_ssem.at[i], ls_rsem.at[i], (source, s)
-        ).wait_recv()
+    sums_done = all_of(ls.at[pl.ds(0, 7)], ls_sem.at[0], ls_sem.at[1])
+    sums_done.wait_recv()
     mean = ls[0]
     for k in range(1, NTM):
         mean = mean + ls[k]
@@ -243,15 +241,7 @@
     spec5 = spec.reshape(NTM, F, 2, LB, PTS)
 
     for f2 in range(2):
-        for i, o in enumerate(GROUP):
-            source = group_source(o)
-            remote(
-                sb.at[source],
-                rb.at[f2, pl.ds(pl.multiple_of(source * 16, 16), 16), :],
-                fs_sem.at[f2, i],
-                fr_sem.at[f2, i],
-                (source, s),
-            ).wait_recv()
+        all_of(rb.at[f2, pl.ds(0, 7 * 16)], fs_sem.at[0], fs_sem.at[1 + f2]).wait_recv()
         real, imag = cs[4 * t + 2 * f2], cs[4 * t + 2 * f2 + 1]
 
         def gather(k, carry):
@@ -296,8 +286,8 @@
             remote(
                 gs.at[f2, oz * 2 + ox // 2],
                 gr.at[k],
-                ga_ssem.at[k],
-                ga_rsem.at[k],
+                ga_sem.at[0],
+                ga_sem.at[1],
                 (t, oz * 4 + ox),
             ).start()
 
@@ -309,62 +299,56 @@
             send_rows(len(HALF))
 
         if f2 == 0:
-            for i, o in enumerate(GROUP):
+            for o in GROUP:
                 other = group_peer(o)
-                copy = remote(
-                    spec5.at[other], mf.at[:, :, t], ps_sem.at[i], pr_sem.at[i], (other, s)
-                )
-                copy.start()
-                sends.append(copy)
+                remote(
+                    spec5.at[other], mf.at[:, :, t], ps_sem.at[0], ps_sem.at[1], (other, s)
+                ).start()
             own_points = pltpu.make_async_copy(spec5.at[t], mf.at[:, :, t], own_sem)
             own_points.start()
 
     rows = gs[h, tile]
-    for i in reversed(range(len(PLANE))):
-        remote(gs.at[0, 0], gr.at[i], ga_ssem.at[i], ga_rsem.at[i], (t, s)).wait_recv()
+    rows_done = all_of(gr.at[pl.ds(0, len(PLANE))], ga_sem.at[0], ga_sem.at[1])
+    rows_done.wait_recv()
+    for i in range(len(PLANE)):
         rows = rows + gr[i]
     gt[tile] = rows
 
-    for i, o in enumerate(HALF):
-        copy = remote(
-            gt.at[tile], gt.at[tile], gb_ssem.at[i], gb_rsem.at[i], (t, plane_peer(o))
-        )
-        copy.start()
-        sends.append(copy)
-    for i, o in enumerate(HALF):
-        oz, ox = (z + 8 - o[0]) % 8, (x + 4 - o[1]) % 4
-        source = oz * 2 + ox // 2
+    for o in HALF:
+        remote(gt.at[tile], gt.at[tile], gb_sem.at[0], gb_sem.at[1], (t, plane_peer(o))).start()
+    tiles_done = all_of(gt.at[pl.ds(0, len(HALF))], gb_sem.at[0], gb_sem.at[1])
+    tiles_done.wait_recv()
+
+    mine = 2 * t + h
+
+    def send_half(part):
+        half_rows = pl.ds(8 * part, 8)
+        for slot in (2, 1, 0, 6, 5, 4, 3):
+            dy = OFFSET_Y[slot]
+            other_y = (y + dy) % 4
+            if slot < 3:
+                column = s
+            else:
+                d = (y + other_y) % 4
+                dx = jnp.where(d == 0, 1, jnp.where(d == 1, 3, 0))
+                dz = jnp.where(d == 2, 1, jnp.where(d == 3, 7, 0))
+                column = ((z + dz) % 8) * 4 + (x + dx) % 4
+            remote(
+                w.at[half_rows],
+                wa.at[mine, half_rows],
+                w_ssem,
+                w_rsem.at[part, slot],
+                (other_y * 2 + core, column),
+            ).start()
         remote(
-            gt.at[tile], gt.at[source], gb_ssem.at[i], gb_rsem.at[i], (t, oz * 4 + ox)
-        ).wait_recv()
-
-    factor(gt, w)
-
-    mine = 2 * t + h
-    for slot in (2, 6, 5, 4, 1, 0, 3):
-        dy = OFFSET_Y[slot]
-        other_y = (y + dy) % 4
-        if slot < 3:
-            column = s
-        else:
-            d = (y + other_y) % 4
-            dx = jnp.where(d == 0, 1, jnp.where(d == 1, 3, 0))
-            dz = jnp.where(d == 2, 1, jnp.where(d == 3, 7, 0))
-            column = ((z + dz) % 8) * 4 + (x + dx) % 4
-        copy = remote(
-            w, wa.at[mine], w_ssem.at[slot], w_rsem.at[slot], (other_y * 2 + core, column)
-        )
-        copy.start()
-        sends.append(copy)
-    copy = remote(w, wa.at[mine], r_ssem.at[7], r_rsem.at[7], (sibling, s))
-    copy.start()
-    sends.append(copy)
+            w.at[half_rows], wa.at[mine, half_rows], r_ssem, r_rsem.at[part, 7], (sibling, s)
+        ).start()
+
+    factor(gt, w, lambda: send_half(0))
+    send_half(1)
     own_points.wait()
-    for i, o in enumerate(GROUP):
-        source = group_source(o)
-        remote(
-            spec5.at[source], mf.at[:, :, source], ps_sem.at[i], pr_sem.at[i], (source, s)
-        ).wait_recv()
+    points_done = all_of(mf.at[:, :, pl.ds(0, 7)], ps_sem.at[0], ps_sem.at[1])
+    points_done.wait_recv()
     row = lax.broadcasted_iota(jnp.int32, (128, 128), 0)
     col = lax.broadcasted_iota(jnp.int32, (128, 128), 1)
 
@@ -392,22 +376,32 @@
         half = jnp.where(turn < 3, h, 1 - h)
         return 4 * ((y + 4 - dy) % 4) + 2 * of_core + half
 
-    for slot in order:
+    def relay(slot, part):
         f = frequency(slot, core)
-        remote(w, wa.at[f], w_ssem.at[slot], w_rsem.at[slot], (sibling, s)).wait_recv()
-        copy = remote(wa.at[f], wa.at[f], r_ssem.at[slot], r_rsem.at[slot], (sibling, s))
-        copy.start()
-        sends.append(copy)
-        multiply(f, wa[f])
+        half_rows = wa.at[f, pl.ds(8 * part, 8)]
+        remote(half_rows, half_rows, w_ssem, w_rsem.at[part, slot], (sibling, s)).wait_recv()
+        remote(half_rows, half_rows, r_ssem, r_rsem.at[part, slot], (sibling, s)).start()
+
+    for slots in (order[:3], order[3:]):
+        for slot in slots:
+            relay(slot, 0)
+        for slot in slots:
+            relay(slot, 1)
+            f = frequency(slot, core)
+            multiply(f, wa[f])
     for i in range(8):
         slot = order[i - 1] if i else 7
         f = frequency(slot, 1 - core) if i else 4 * y + 2 * (1 - core) + h
-        remote(w, wa.at[f], r_ssem.at[slot], r_rsem.at[slot], (sibling, s)).wait_recv()
+        for part in range(2):
+            half_rows = wa.at[f, pl.ds(8 * part, 8)]
+            remote(half_rows, half_rows, r_ssem, r_rsem.at[part, slot], (sibling, s)).wait_recv()
         multiply(f, wa[f])
-    for k in range(len(PLANE)):
-        remote(gs.at[0, 0], gr.at[k], ga_ssem.at[k], ga_rsem.at[k], (t, s)).wait_send()
-    for copy in sends:
-        copy.wait_send()
+
+    for done in (sums_done, rows_done, tiles_done, points_done):
+        done.wait_send()
+    all_of(sb.at[pl.ds(0, 14)], fs_sem.at[0], fs_sem.at[1]).wait_send()
+    all_of(wa.at[pl.ds(0, 7)], w_ssem, w_ssem).wait_send()
+    all_of(wa.at[pl.ds(0, 8)], r_ssem, r_ssem).wait_send()
 
 
 def hand_out(rfac, modes, rfac_out, modes_out, sems):
@@ -448,20 +442,15 @@
             vmem((F, 2, NTM, LB, PTS), f32),
             dma,
             dma((CHUNKS,)),
+            dma((3,)),
+            dma((2,)),
+            dma((2,)),
+            dma((2,)),
+            dma((2,)),
+            dma,
             dma((2, 7)),
-            dma((2, 7)),
-            dma((7,)),
-            dma((7,)),
-            dma((7,)),
-            dma((7,)),
-            dma((NSPACE,)),
-            dma((NSPACE,)),
-            dma((16,)),
-            dma((16,)),
-            dma((7,)),
-            dma((7,)),
-            dma((8,)),
-            dma((8,)),
+            dma,
+            dma((2, 8)),
             dma,
             pltpu.SemaphoreType.REGULAR,
             pltpu.SemaphoreType.REGULAR,

time: 45.9 us -> 44.3 us (0.965)
  Pallas kernels: 45.2 us -> 43.6 us
    pallas_call x1, Pallas kernels: 43.8 us -> 42.2 us  [shards(): pl.pallas_call(functools.partial(main_kernel, [float(v) for v in colsum])...]
where the time goes in v4:
time: 44.3 us; the launch traced here: 44.2 us
  Pallas kernels  43.6 us (98%)
  between operations  0.64 us (1%)
    pallas_call x1, Pallas kernels, shards(): pl.pallas_call(functools.partial(main_kernel, [float(v) for v in colsum])...  42.2 us
    pallas_call x1, Pallas kernels, shards(): pl.pallas_call(hand_out, out_shape=(jax.ShapeDtypeStruct((F, 128, 128), f...  1.33 us

profile of v4, /device:TPU:1, one launch (start us, length us, event | category | flops | bytes accessed | tf_op | source)
XLA Modules:
  0.0 44.2 jit_solution(17483407299150517363)
XLA Ops:
  0.6 42.2 %factors.1 = (f32[16,128,128]{2,1,0:T(8,128)S(1)}, f32[16,128,128]{2,1,0:T(8,128)S(1)}) custom-call(bf16[2048,1024]{1,0:T(8,128)(2,1)} %data.1, f32[48,256]{1,0:T(8,128)} %constant.2.clone.tab_hbm), custom_call_target="tpu_custom_call" | custom-call | tf_op jit(solution)/shard_map/factors/pallas_call | solution.py:423
  42.9 1.3 %hand_out.1 = (f32[16,128,128]{2,1,0:T(8,128)}, f32[16,128,128]{2,1,0:T(8,128)}) custom-call(f32[16,128,128]{2,1,0:T(8,128)S(1)} %get-tuple-element.4.rfac, f32[16,128,128]{2,1,0:T(8,128)S(1)} %get-tuple-element.5.modes), custom_call_target="tpu_custom_call" | custom-call | tf_op jit(solution)/shard_map/hand_out/pallas_call | solution.py:463

commit v5 on v4

--- a/solution.py
+++ b/solution.py
@@ -69,7 +69,7 @@
             inverses.append(inv)
             cross.append(here)
         w_ref[k] = own * lax.rsqrt(diag)
-        if k == 7:
+        if k == 11:
             half_done()
         for j in range(k + 1, 16):
             rest = w_ref[j]
@@ -92,6 +92,7 @@
     key=lambda o: -plane_distance(*o),
 )
 OFFSET_Y = (1, 3, 2, 0, 1, 3, 2)
+PARTS = ((0, 12), (12, 4))
 HALF = [o for o in PLANE if sum(o) % 2 == 0]
 OTHER = [o for o in PLANE if sum(o) % 2 == 1]
 GROUP = [(2, 0), (2, 1), (1, 0), (3, 0), (1, 1), (3, 1), (0, 1)]
@@ -146,7 +147,7 @@
     def signal(sem, device):
         pl.semaphore_signal(sem, inc=1, device_id=device, device_id_type=MESH)
 
-    for dy in range(4):
+    for dy in (2, 1, 3, 0):
         other = ((y + dy) % 4) * 2
         if dy == 0:
 
@@ -245,17 +246,23 @@
         real, imag = cs[4 * t + 2 * f2], cs[4 * t + 2 * f2 + 1]
 
         def gather(k, carry):
-            shift = ls[k] * (NTM / NT) - mean
             for r in range(8):
                 lanes = pl.ds(r * 128, 128)
-                block = rb[f2, pl.ds(pl.multiple_of(k * 16, 16), 16), lanes].astype(jnp.float32)
-                row = jnp.broadcast_to(shift[r : r + 1, :], (8, 128))
-                mat[pl.ds(pl.multiple_of(k * 8, 8), 8), lanes] = block[:8] + real * row
-                mat[pl.ds(pl.multiple_of(64 + k * 8, 8), 8), lanes] = block[8:] + imag * row
+                pieces = []
+                for n in range(2):
+                    source = 2 * k + n
+                    shift = ls[source, pl.ds(r, 1), :] * (NTM / NT) - mean[r : r + 1, :]
+                    block = rb[f2, pl.ds(pl.multiple_of(source * 16, 16), 16), lanes]
+                    block = block.astype(jnp.float32)
+                    pieces.append((block[:8] + real * shift, block[8:] + imag * shift))
+                for part in range(2):
+                    mat[pl.ds(pl.multiple_of(part * 64 + k * 16, 16), 16), lanes] = jnp.concatenate(
+                        [piece[part] for piece in pieces], axis=0
+                    ).astype(jnp.bfloat16)
             return carry
 
-        lax.fori_loop(0, NTM, gather, 0)
-        rounded = mat[...].astype(jnp.bfloat16)
+        lax.fori_loop(0, NTM // 2, gather, 0)
+        rounded = mat[...]
         gram = lax.dot_general(
             rounded, rounded, (((1,), (1,)), ((), ())), preferred_element_type=jnp.float32
         ) * (1.0 / NX)
@@ -298,7 +305,7 @@
         def _():
             send_rows(len(HALF))
 
-        if f2 == 0:
+        if f2 == 1:
             for o in GROUP:
                 other = group_peer(o)
                 remote(
@@ -322,7 +329,7 @@
     mine = 2 * t + h
 
     def send_half(part):
-        half_rows = pl.ds(8 * part, 8)
+        half_rows = pl.ds(*PARTS[part])
         for slot in (2, 1, 0, 6, 5, 4, 3):
             dy = OFFSET_Y[slot]
             other_y = (y + dy) % 4
@@ -378,7 +385,7 @@
 
     def relay(slot, part):
         f = frequency(slot, core)
-        half_rows = wa.at[f, pl.ds(8 * part, 8)]
+        half_rows = wa.at[f, pl.ds(*PARTS[part])]
         remote(half_rows, half_rows, w_ssem, w_rsem.at[part, slot], (sibling, s)).wait_recv()
         remote(half_rows, half_rows, r_ssem, r_rsem.at[part, slot], (sibling, s)).start()
 
@@ -387,13 +394,14 @@
             relay(slot, 0)
         for slot in slots:
             relay(slot, 1)
+        for slot in slots:
             f = frequency(slot, core)
             multiply(f, wa[f])
     for i in range(8):
         slot = order[i - 1] if i else 7
         f = frequency(slot, 1 - core) if i else 4 * y + 2 * (1 - core) + h
         for part in range(2):
-            half_rows = wa.at[f, pl.ds(8 * part, 8)]
+            half_rows = wa.at[f, pl.ds(*PARTS[part])]
             remote(half_rows, half_rows, r_ssem, r_rsem.at[part, slot], (sibling, s)).wait_recv()
         multiply(f, wa[f])
 
@@ -433,7 +441,7 @@
             vmem((F, 2 * LB, COLS), bf16),
             vmem((2, 2 * NB, COLS), bf16),
             vmem((NTM, 8, 128), f32),
-            vmem((2 * NB, COLS), f32),
+            vmem((2 * NB, COLS), bf16),
             vmem((2, 16, 8, 128), f32),
             vmem((NSPACE, 8, 128), f32),
             vmem((16, 8, 128), f32),

time: 44.3 us -> 44.1 us (level)
  no operation moved by 1% of the time
where the time goes in v5:
time: 44.1 us; the launch traced here: 44 us
  Pallas kernels  43.4 us (98%)
  between operations  0.64 us (1%)
    pallas_call x1, Pallas kernels, shards(): pl.pallas_call(functools.partial(main_kernel, [float(v) for v in colsum])...  42 us
    pallas_call x1, Pallas kernels, shards(): pl.pallas_call(hand_out, out_shape=(jax.ShapeDtypeStruct((F, 128, 128), f...  1.33 us

profile of v5, /device:TPU:1, one launch (start us, length us, event | category | flops | bytes accessed | tf_op | source)
XLA Modules:
  0.0 44.0 jit_solution(18389051953673777945)
XLA Ops:
  0.6 42.0 %factors.1 = (f32[16,128,128]{2,1,0:T(8,128)S(1)}, f32[16,128,128]{2,1,0:T(8,128)S(1)}) custom-call(bf16[2048,1024]{1,0:T(8,128)(2,1)} %data.1, f32[48,256]{1,0:T(8,128)} %constant.2.clone.tab_hbm), custom_call_target="tpu_custom_call" | custom-call | tf_op jit(solution)/shard_map/factors/pallas_call | solution.py:431
  42.7 1.3 %hand_out.1 = (f32[16,128,128]{2,1,0:T(8,128)}, f32[16,128,128]{2,1,0:T(8,128)}) custom-call(f32[16,128,128]{2,1,0:T(8,128)S(1)} %get-tuple-element.4.rfac, f32[16,128,128]{2,1,0:T(8,128)S(1)} %get-tuple-element.5.modes), custom_call_target="tpu_custom_call" | custom-call | tf_op jit(solution)/shard_map/hand_out/pallas_call | solution.py:471

commit v6 on v5

--- a/solution.py
+++ b/solution.py
@@ -113,6 +113,41 @@
     tile = z * 2 + x // 2
     sibling = 2 * y + 1 - core
 
+    def remote(src, dst, send_sem, recv_sem, device):
+        return pltpu.make_async_remote_copy(
+            src_ref=src,
+            dst_ref=dst,
+            send_sem=send_sem,
+            recv_sem=recv_sem,
+            device_id=device,
+            device_id_type=MESH,
+        )
+
+    def group_peer(o):
+        return ((y + o[0]) % 4) * 2 + (core + o[1]) % 2
+
+    def group_source(o):
+        return ((y + 4 - o[0]) % 4) * 2 + (core + o[1]) % 2
+
+    def plane_peer(o):
+        return ((z + o[0]) % 8) * 4 + (x + o[1]) % 4
+
+    barrier = pltpu.get_barrier_semaphore()
+
+    def signal(sem, device):
+        pl.semaphore_signal(sem, inc=1, device_id=device, device_id_type=MESH)
+
+    for dy in (2, 1, 3, 0):
+        other = ((y + dy) % 4) * 2
+        if dy == 0:
+
+            @pl.when(core == 1)
+            def _():
+                signal(barrier, (other, s))
+
+        else:
+            signal(barrier, (other, s))
+
     load_tab = pltpu.make_async_copy(tab_hbm, tab, tab_sem)
     load_tab.start()
     loads = []
@@ -122,41 +157,6 @@
         )
         copy.start()
         loads.append(copy)
-
-    def remote(src, dst, send_sem, recv_sem, device):
-        return pltpu.make_async_remote_copy(
-            src_ref=src,
-            dst_ref=dst,
-            send_sem=send_sem,
-            recv_sem=recv_sem,
-            device_id=device,
-            device_id_type=MESH,
-        )
-
-    def group_peer(o):
-        return ((y + o[0]) % 4) * 2 + (core + o[1]) % 2
-
-    def group_source(o):
-        return ((y + 4 - o[0]) % 4) * 2 + (core + o[1]) % 2
-
-    def plane_peer(o):
-        return ((z + o[0]) % 8) * 4 + (x + o[1]) % 4
-
-    barrier = pltpu.get_barrier_semaphore()
-
-    def signal(sem, device):
-        pl.semaphore_signal(sem, inc=1, device_id=device, device_id_type=MESH)
-
-    for dy in (2, 1, 3, 0):
-        other = ((y + dy) % 4) * 2
-        if dy == 0:
-
-            @pl.when(core == 1)
-            def _():
-                signal(barrier, (other, s))
-
-        else:
-            signal(barrier, (other, s))
 
     for j in range(2 * F):
         cs[j] = jnp.float32(colsum[j])
@@ -330,7 +330,7 @@
 
     def send_half(part):
         half_rows = pl.ds(*PARTS[part])
-        for slot in (2, 1, 0, 6, 5, 4, 3):
+        for slot in (6, 2, 5, 4, 1, 0, 3):
             dy = OFFSET_Y[slot]
             other_y = (y + dy) % 4
             if slot < 3:

time: 44.1 us -> 44.1 us (level)
  no operation moved by 1% of the time
where the time goes in v6:
time: 44.1 us; the launch traced here: 44 us
  Pallas kernels  43.4 us (98%)
  between operations  0.64 us (1%)
    pallas_call x1, Pallas kernels, shards(): pl.pallas_call(functools.partial(main_kernel, [float(v) for v in colsum])...  42.1 us
    pallas_call x1, Pallas kernels, shards(): pl.pallas_call(hand_out, out_shape=(jax.ShapeDtypeStruct((F, 128, 128), f...  1.33 us

profile of v6, /device:TPU:1, one launch (start us, length us, event | category | flops | bytes accessed | tf_op | source)
XLA Modules:
  0.0 44.0 jit_solution(12001667128475661178)
XLA Ops:
  0.6 42.1 %factors.1 = (f32[16,128,128]{2,1,0:T(8,128)S(1)}, f32[16,128,128]{2,1,0:T(8,128)S(1)}) custom-call(bf16[2048,1024]{1,0:T(8,128)(2,1)} %data.1, f32[48,256]{1,0:T(8,128)} %constant.2.clone.tab_hbm), custom_call_target="tpu_custom_call" | custom-call | tf_op jit(solution)/shard_map/factors/pallas_call | solution.py:431
  42.7 1.3 %hand_out.1 = (f32[16,128,128]{2,1,0:T(8,128)}, f32[16,128,128]{2,1,0:T(8,128)}) custom-call(f32[16,128,128]{2,1,0:T(8,128)S(1)} %get-tuple-element.4.rfac, f32[16,128,128]{2,1,0:T(8,128)S(1)} %get-tuple-element.5.modes), custom_call_target="tpu_custom_call" | custom-call | tf_op jit(solution)/shard_map/hand_out/pallas_call | solution.py:471
